TPU v7x, 256 devices: a whole 4x4x8 slice. The times are simulated.
256 devices in a mesh: group: 2 (over z_hi), rows: 8 (over z_lo, core), dp: 16 (over x, y).
Axes of the slice: x: 4, y: 4, z: 8 (z_hi: 2, z_lo: 4; z = z_hi * 4 + z_lo), core: 2. Of those that a mesh axis runs over, the one named last changes fastest.
Arguments:
- teacher_tokens: bfloat16 [65536, 1536], P(('rows', 'dp')), may hold values from -40 to 40
- teacher_qkv: bfloat16 [1536, 4608], P('rows'), may hold values from -20 to 20
- teacher_out: bfloat16 [1536, 1536], P('rows'), may hold values from -0.15625 to 0.15625
- student_tokens: bfloat16 [65536, 1024], P(('rows', 'dp')), may hold values from -40 to 40
- student_weights: bfloat16 [1024, 4096], P('rows'), may hold values from -20 to 20
Outputs:
- student_grad: float32 [1024, 4096], P(('group', 'rows'), 'dp')
All inputs are finite; a program needn't handle non-finite values.
Results may differ from a plain program's by a relative error of at most 0.009.
Values may be sent and summed in bfloat16 or wider, within the bound.
A program may use at most 128 MiB of HBM per device.

v0:
```python
import jax
import jax.numpy as jnp
from jax import lax
from jax.sharding import PartitionSpec as P

HEAD = 64
IMG_TOK = 256


epsilon = 1e-06
distill_weight = 512.0


def shifted(value, axis, steps):
    count = lax.axis_size(axis)
    initial, last = (max(0, -steps), min(count, count - steps))
    return lax.ppermute(value, axis, [(source, source + steps) for source in range(initial, last)])


def normed(tokens):
    values = tokens.astype(jnp.float32)
    centred = values - jnp.mean(values, axis=-1, keepdims=True)
    spread = jnp.mean(centred * centred, axis=-1, keepdims=True)
    return (centred * lax.rsqrt(spread + epsilon)).astype(jnp.bfloat16)


def attention_fwd(qkv_act, model_width, head_size):
    images = qkv_act.shape[0] // IMG_TOK
    head_count = model_width // head_size
    shaped = qkv_act.reshape(images, IMG_TOK, 3, head_count, head_size)
    queries = shaped[:, :, 0]
    keys_b = shaped[:, :, 1]
    values_b = shaped[:, :, 2]
    scores = jnp.einsum(
        "bihe,bjhe->bhij", queries, keys_b, preferred_element_type=jnp.float32
    ) * head_size ** (-0.5)
    scores = scores - jnp.max(scores, axis=-1, keepdims=True)
    exps_raw = jnp.exp(scores)
    softmax_out = exps_raw / jnp.sum(exps_raw, axis=-1, keepdims=True)
    probs_b = softmax_out.astype(jnp.bfloat16)
    mixed_out = jnp.einsum("bhij,bjhe->bihe", probs_b, values_b, preferred_element_type=jnp.float32)
    return (
        mixed_out.reshape(qkv_act.shape[0], model_width).astype(jnp.bfloat16),
        softmax_out,
        probs_b,
    )


def attention_bwd(qkv_act, softmax_out, probs_b, mixed_grad, model_width, head_size):
    images = qkv_act.shape[0] // IMG_TOK
    head_count = model_width // head_size
    shaped = qkv_act.reshape(images, IMG_TOK, 3, head_count, head_size)
    queries = shaped[:, :, 0]
    keys_b = shaped[:, :, 1]
    values_b = shaped[:, :, 2]
    upstream = mixed_grad.reshape(images, IMG_TOK, head_count, head_size)
    prob_grad = jnp.einsum(
        "bihe,bjhe->bhij", upstream, values_b, preferred_element_type=jnp.float32
    )
    value_grad = jnp.einsum(
        "bhij,bihe->bjhe", probs_b, upstream, preferred_element_type=jnp.float32
    ).astype(jnp.bfloat16)
    row_total = jnp.sum(prob_grad * softmax_out, axis=-1, keepdims=True)
    score_grad = (softmax_out * (prob_grad - row_total) * head_size ** (-0.5)).astype(jnp.bfloat16)
    query_grad = jnp.einsum(
        "bhij,bjhe->bihe", score_grad, keys_b, preferred_element_type=jnp.float32
    ).astype(jnp.bfloat16)
    key_grad = jnp.einsum(
        "bhij,bihe->bjhe", score_grad, queries, preferred_element_type=jnp.float32
    ).astype(jnp.bfloat16)
    stacked = jnp.stack([query_grad, key_grad, value_grad], axis=2)
    return stacked.reshape(qkv_act.shape[0], 3 * model_width)


def gram_of(features):
    model_width = features.shape[1]
    row_scale = lax.rsqrt(
        jnp.mean(features * features, axis=-1, keepdims=True) + epsilon
    ) * model_width ** (-0.5)
    unit_rows = (features * row_scale).reshape(-1, IMG_TOK, model_width)
    return jnp.einsum("bic,bjc->bij", unit_rows, unit_rows, precision=lax.Precision.HIGHEST)


def output_grad(student_result, teacher_gram, weight):

    def loss_of(result_rows):
        difference = gram_of(result_rows) - teacher_gram
        return weight * jnp.sum(difference * difference)

    primal, pullback = jax.vjp(loss_of, student_result)
    return pullback(jnp.ones_like(primal))[0].astype(jnp.bfloat16)


def per_device(teacher_tokens, teacher_qkv, teacher_out, student_tokens, student_weights):
    group_index = lax.axis_index("group")
    is_teacher = group_index == 0
    is_student = group_index == 1
    rows_here = teacher_tokens.shape[0]
    width_t = teacher_tokens.shape[1]
    width_s = student_tokens.shape[1]
    images_here = rows_here // IMG_TOK
    weight = distill_weight / (images_here * lax.axis_size("rows") * lax.axis_size("dp"))
    row_block = width_s // (2 * lax.axis_size("rows"))
    col_block = 4 * width_s // lax.axis_size("dp")
    normed_t = normed(teacher_tokens)
    running = jnp.zeros((rows_here, 3 * width_t), jnp.float32)
    shard_rows = lax.all_gather(teacher_qkv, "rows", axis=0, tiled=True)

    def product():
        return jnp.dot(normed_t, shard_rows, preferred_element_type=jnp.float32)

    act_t = lax.cond(is_teacher, product, lambda: running).astype(jnp.bfloat16)

    def mix_teacher():
        return attention_fwd(act_t, width_t, HEAD)[0]

    def mix_quiet():
        return jnp.zeros((rows_here, width_t), jnp.bfloat16)

    mixed_t = lax.cond(is_teacher, mix_teacher, mix_quiet)
    add_running = jnp.zeros((rows_here, width_t), jnp.float32)
    add_shard_rows = lax.all_gather(teacher_out, "rows", axis=0, tiled=True)

    def product():
        return jnp.dot(mixed_t, add_shard_rows, preferred_element_type=jnp.float32)

    projected = lax.cond(is_teacher, product, lambda: add_running)
    features_here = (teacher_tokens.astype(jnp.float32) + projected).astype(jnp.bfloat16)
    arrived = shifted(features_here, "group", 1)
    gathered = lax.all_gather(student_weights, "rows", axis=0, tiled=True)
    term_rows = width_s * 4 * width_s // col_block

    def student_terms():
        w_qkv = gathered[:, : 3 * width_s]
        w_out = gathered[:, 3 * width_s :]
        normed_s = normed(student_tokens)
        act_s = jnp.dot(normed_s, w_qkv, preferred_element_type=jnp.float32).astype(jnp.bfloat16)
        mixed_s, softmax_out, probs_b = attention_fwd(act_s, width_s, HEAD)
        result_s = student_tokens.astype(jnp.float32) + jnp.dot(
            mixed_s, w_out, preferred_element_type=jnp.float32
        )
        out_grad = output_grad(result_s, gram_of(arrived.astype(jnp.float32)), weight)
        mixed_grad = jnp.einsum(
            "tc,dc->td", out_grad, w_out, preferred_element_type=jnp.float32
        ).astype(jnp.bfloat16)
        act_grad = attention_bwd(act_s, softmax_out, probs_b, mixed_grad, width_s, HEAD)
        left_in = normed_s.reshape(rows_here, 2, width_s // (2 * row_block), row_block)
        left_mid = mixed_s.reshape(rows_here, 2, width_s // (2 * row_block), row_block)
        right_in = act_grad.reshape(rows_here, 3 * width_s // col_block, col_block)
        right_out = out_grad.reshape(rows_here, width_s // col_block, col_block)
        grad_terms = jnp.concatenate(
            [
                jnp.einsum(
                    "tgra,tdb->rdgab", left_in, right_in, preferred_element_type=jnp.float32
                ),
                jnp.einsum(
                    "tgra,tdb->rdgab", left_mid, right_out, preferred_element_type=jnp.float32
                ),
            ],
            axis=1,
        )
        return grad_terms.reshape(term_rows, col_block)

    def quiet_terms():
        return jnp.zeros((term_rows, col_block), jnp.float32)

    local_terms = lax.cond(is_student, student_terms, quiet_terms)
    grad_slab = lax.psum_scatter(local_terms, ("rows", "dp"), scatter_dimension=0, tiled=True)
    returned = shifted(grad_slab[:row_block], "group", -1)
    return jnp.where(is_teacher, returned, grad_slab[row_block:])


def solution(mesh):
    return jax.shard_map(
        per_device,
        mesh=mesh,
        in_specs=(
            P(("rows", "dp"), None),
            P("rows", None),
            P("rows", None),
            P(("rows", "dp"), None),
            P("rows", None),
        ),
        out_specs=P(("group", "rows"), "dp"),
        check_vma=False,
    )
```

profile of v0, /device:TPU:4, one launch (start us, length us, event | category | flops | bytes accessed | tf_op | source)
XLA Modules:
  0.0 1213.6 jit_solution(6840471683234780114)
XLA Ops:
  10.1 150.1 %all-gather.6.cloned.1.call-done = bf16[1536,4608]{1,0:T(8,128)(2,1)} async-done(((bf16[192,4608]{1,0:T(8,128)(2,1)}), bf16[1536,4608]{1,0:T(8,128)(2,1)}) %all-gather.6.cloned.1.call-update) | async-done | bytes 14155792 | tf_op jit(solution)/shard_map/all_gather | solution.py:107
  160.2 14.1 %conditional.4 = (bf16[512,4608]{1,0:T(8,128)(2,1)}) conditional(s32[]{:T(128)} %convert_element_type.97, () %tuple.36, (bf16[512,1536]{1,0:T(8,128)(2,1)S(1)}, bf16[1536,4608]{1,0:T(8,128)(2,1)}) %tuple.37), branch_computations={%region_2.0_spmd, %region_3.0_spmd} | conditional | flops 7250116608 | bytes 20447240 | solution.py:112
  160.2 14.1 %convolution_convert_fusion = bf16[512,4608]{1,0:T(8,128)(2,1)} fusion(bf16[512,1536]{1,0:T(8,128)(2,1)S(1)} %get-tuple-element.32, bf16[1536,4608]{1,0:T(8,128)(2,1)} %get-tuple-element.34), kind=kOutput, calls=%fused_computation | convolution fusion | flops 7250116608 | bytes 20447232 | tf_op jit(solution)/shard_map/cond/branch_1_fun/dot_general | solution.py:110
  174.3 63.3 %conditional.5 = (bf16[512,1536]{0,1:T(8,128)(2,1)S(1)}) conditional(s32[]{:T(128)} %convert_element_type.97, () %tuple.35, bf16[512,4608]{1,0:T(8,128)(2,1)} %get-tuple-element.56), branch_computations={%region_4.0_spmd, %region_5.0_spmd} | conditional | flops 824967424 | bytes 91324424 | solution.py:120
  174.8 12.6 %reshape.101 = bf16[2,256,3,24,64]{4,3,2,1,0:T(8,128)(2,1)} reshape(bf16[512,4608]{1,0:T(8,128)(2,1)} %param.3) | data formatting | bytes 9437184 | tf_op jit(solution)/shard_map/cond/branch_1_fun/reshape | solution.py:30
  187.5 6.9 fusion.104
  194.4 3.4 copy.66
  197.8 4.5 copy.67
  202.3 7.8 fusion.8
  210.1 15.9 %fusion.105 = (f32[2,24,256]{2,1,0:T(8,128)S(1)}, f32[2,24,256,256]{2,3,1,0:T(8,128)}) fusion(f32[2,24,256,256]{2,3,1,0:T(8,128)} %fusion.8), kind=kOutput, calls=%fused_computation.108 | output fusion | flops 12583167 | bytes 25214976 | tf_op jit(solution)/shard_map/cond/branch_1_fun/sub | solution.py:37
  226.0 3.4 copy.65
  229.5 6.1 fusion.11
  235.6 1.6 copy.24
  237.6 6.9 conditional.6
  237.8 6.7 fusion.108
  244.5 3.6 fusion.103
  248.1 1.4 collective-permute-start
  249.5 126.4 %all-gather.4.cloned.1.call-done = bf16[1024,4096]{1,0:T(8,128)(2,1)} async-done(((bf16[128,4096]{1,0:T(8,128)(2,1)}), bf16[1024,4096]{1,0:T(8,128)(2,1)}) %all-gather.4.cloned.1.call-update) | async-done | bytes 8388624 | tf_op jit(solution)/shard_map/all_gather | solution.py:130
  375.9 7.1 conditional.7
  375.9 6.0 broadcast.115
  383.0 811.4 %reduce-scatter.2.cloned.1.call-done = f32[128,256]{1,0:T(8,128)} async-done(((f32[16384,256]{1,0:T(8,128)}), f32[128,256]{1,0:T(8,128)}) %reduce-scatter.2.cloned.1.call-update) | async-done | bytes 131088 | tf_op jit(solution)/shard_map/reduce_scatter | solution.py:168
  1195.2 1.3 collective-permute-start.1
  1196.5 8.8 collective-permute-done.1
  1205.3 1.5 slice_select_fusion
  (21 shorter events, 4.7 us)
Async XLA Ops:
  6.5 2.3 copy-start
  6.5 153.7 %all-gather.6.cloned.1.call-start = ((), (), s32[]{:S(2)}) async-start(), calls=%async_computation.2 | async-start | bytes 15925248 | tf_op jit(solution)/shard_map/all_gather | solution.py:107
  7.3 230.3 %all-gather.8.cloned.1.call-start = ((), (), s32[]{:S(2)}) async-start(), calls=%async_computation.3 | async-start | bytes 5308416 | tf_op jit(solution)/shard_map/all_gather | solution.py:122
  8.0 367.9 %all-gather.4.cloned.1.call-start = ((), (), s32[]{:S(2)}) async-start(), calls=%async_computation.1 | async-start | bytes 9437184 | tf_op jit(solution)/shard_map/all_gather | solution.py:130
  8.7 1185.6 %reduce-scatter.2.cloned.1.call-start = ((), (), s32[]{:S(2)}) async-start(), calls=%async_computation.4 | async-start | bytes 16908288 | tf_op jit(solution)/shard_map/reduce_scatter | solution.py:168
  244.5 131.4 %copy-start.2 = (bf16[512,1024]{1,0:T(8,128)(2,1)S(1)}, bf16[512,1024]{1,0:T(8,128)(2,1)}, u32[]{:S(2)}) copy-start(bf16[512,1024]{1,0:T(8,128)(2,1)} %param.16) | copy-start | bytes 3145732
  248.1 127.8 %collective-permute-start = (bf16[512,1536]{1,0:T(8,128)(2,1)}, bf16[512,1536]{1,0:T(8,128)(2,1)S(1)}, u32[]{:S(2)}, u32[]{:S(2)}) collective-permute-start(bf16[512,1536]{1,0:T(8,128)(2,1)} %fusion.103), channel_id=1, source_target_pairs={{0,128},{1,129},{2,130},{3,131},{4,132},{5,133},{6,134},{7,135},{8... | collective-permute-start | bytes 4718600 | tf_op jit(solution)/shard_map/ppermute | solution.py:17
  1195.2 10.1 collective-permute-start.1
Sparse Core Ops, SparseCore 0:
  9.1 151.0 all-gather.5
  162.0 58.2 all-gather.7
  222.1 153.7 all-gather.3
  383.1 811.1 reduce-scatter.1
where the time goes:
time: 1240 us; the launch traced here: 1210 us
  waiting for transfers between devices  1100 us (89%)
  local copies, waits for them, and re-layouts  39.7 us (3%)
  matrix products  34.8 us (3%)
  other arithmetic  22.3 us (2%)
  between operations  13.5 us (1%)
    reduce_scatter x1, waiting for transfers between devices, per_device(): lax.psum_scatter(local_terms, ('rows', 'dp'), scatter_dimension=0, tiled=...  811 us
    all_gather x1, waiting for transfers between devices, per_device(): shard_rows = lax.all_gather(teacher_qkv, 'rows', axis=0, tiled=True)  150 us
    all_gather x1, waiting for transfers between devices, per_device(): gathered = lax.all_gather(student_weights, 'rows', axis=0, tiled=True)  126 us
  transfers between devices with their start and end apart: 6, of which 4 were waited for; matrix products, arithmetic and copies ran while one was open for 7% of the time, Pallas kernels for 0%

commit v1 on v0

v1 whole, which is shorter than its diff:
```python
import jax
import jax.numpy as jnp
from jax import lax
from jax.experimental import pallas as pl
from jax.experimental.pallas import tpu as pltpu
from jax.sharding import PartitionSpec as P

MESH = pl.DeviceIdType.MESH
BF = jnp.bfloat16
F32 = jnp.float32

T = 256
DT = 1536
DS = 1024
TW = 4 * DT
SW = 4 * DS
RT = DT // 8
RS = DS // 8
QT = RT // 4
QS = RS // 4
EPS = 1e-06
EXP2_SCALE = 0.125 * 1.4426950408889634

CHUNKS = (
    [(True, 768 * i, 768) for i in range(6)]
    + [(False, 1024 * i, 1024) for i in range(3)]
    + [(True, 4608 + 768 * i, 768) for i in range(2)]
    + [(False, 3072, 1024)]
)
NC = len(CHUNKS)


def mm(a, b, ca=1, cb=0):
    return lax.dot_general(a, b, (((ca,), (cb,)), ((), ())), preferred_element_type=F32)


def kernel(
    tt, tq, to, st, sw, out,
    Wt, Ws, xt, xs, nt, ns, at, mt, as_, pr, ms, gt, tr, lt, rg, mg,
    gp, l1, r1, l2, r2, gp2, bl1, br1, bl2, br2, z3, zr,
    loc_sem, zs_send, zs_recv, a_send, al_recv, ar_recv, b_send, bl_recv, br_recv, c_send, c_recv,
    x_send, x_recv, p1_send, pl1_recv, pr1_recv, pl2_recv, pr2_recv,
    p2_send, ql1_recv, qr1_recv, ql2_recv, qr2_recv, p3_send, p3_recv,
):
    g = lax.axis_index("group")
    r = lax.axis_index("rows")
    d = lax.axis_index("dp")
    zl, c = lax.div(r, 2), lax.rem(r, 2)
    z = g * 4 + zl
    x, y = lax.div(d, 4), lax.rem(d, 4)
    oc = 1 - c
    ma = x * oc + y * c
    mb = y * oc + x * c

    def a_peer(step):
        return {"dp": 4 * lax.rem(x + step * oc, 4) + lax.rem(y + step * c, 4)}

    def b_peer(step):
        return {"dp": 4 * lax.rem(x + step * c, 4) + lax.rem(y + step * oc, 4)}

    def z_peer(step):
        far = lax.rem(z + step, 8)
        return {"group": lax.div(far, 4), "rows": 2 * lax.rem(far, 4) + c}

    sibling = {"rows": r + 1 - 2 * c}

    def send(src, dst, send_sem, recv_sem, to_whom):
        pltpu.make_async_remote_copy(
            src_ref=src, dst_ref=dst, send_sem=send_sem, recv_sem=recv_sem,
            device_id=to_whom, device_id_type=MESH,
        ).start()

    def wait(ref, sem):
        pltpu.make_async_copy(ref, ref, sem).wait()

    local = [
        pltpu.make_async_copy(tt.at[pl.ds(g * T, T)], xt, loc_sem.at[0]),
        pltpu.make_async_copy(st.at[pl.ds(g * T, T)], xs, loc_sem.at[1]),
        pltpu.make_async_copy(tq, Wt.at[zl, c, :, 0:4608], loc_sem.at[2]),
        pltpu.make_async_copy(to, Wt.at[zl, c, :, 4608:6144], loc_sem.at[3]),
        pltpu.make_async_copy(sw, Ws.at[zl, c], loc_sem.at[4]),
    ]
    for copy in local:
        copy.start()

    barrier = pltpu.get_barrier_semaphore()
    peers = [z_peer(s) for s in range(1, 8)] + [a_peer(1), a_peer(3), b_peer(1), b_peer(3), sibling]
    for peer in peers:
        pl.semaphore_signal(barrier, inc=1, device_id=peer, device_id_type=MESH)
    pl.semaphore_wait(barrier, len(peers))

    def piece(chunk, shard, quarter, cols):
        teacher = CHUNKS[chunk][0]
        size = QT if teacher else QS
        rows = pl.ds(pl.multiple_of(quarter * size, 16), size)
        return (Wt if teacher else Ws).at[shard, c, rows, cols]

    def whole(chunk):
        _, first, count = CHUNKS[chunk]
        return slice(first, first + count)

    def half(chunk, which):
        _, first, count = CHUNKS[chunk]
        return slice(first + which * count // 2, first + (which + 1) * count // 2)

    def three(chunk, cols):
        teacher = CHUNKS[chunk][0]
        return (Wt.at[0, 0, 0 : 3 * QT, cols]) if teacher else (Ws.at[0, 0, 0 : 3 * QS, cols])

    def six(chunk, cols):
        teacher = CHUNKS[chunk][0]
        return (Wt.at[0, :, 0 : 3 * QT, cols]) if teacher else (Ws.at[0, :, 0 : 3 * QS, cols])

    def core_half(chunk, core):
        teacher = CHUNKS[chunk][0]
        return (Wt if teacher else Ws).at[:, core, :, whole(chunk)]

    for k in range(NC):
        teacher, first, count = CHUNKS[k]
        size = QT if teacher else QS
        rows = pl.ds(pl.multiple_of(ma * size, 16), size)
        if not teacher:
            src = sw.at[rows, whole(k)]
        elif first < 4608:
            src = tq.at[rows, whole(k)]
        else:
            src = to.at[rows, slice(first - 4608, first - 4608 + count)]
        for step in (1, 7, 2 if k % 2 == 0 else 6):
            send(src, piece(k, zl, ma, whole(k)), zs_send.at[k], zs_recv.at[k], z_peer(step))

    def stage_a(k):
        wait(three(k, whole(k)), zs_recv.at[k])
        for j in (1, 2, 3):
            src = piece(k, lax.rem(zl + j, 4), ma, whole(k))
            send(src, src, a_send.at[k], al_recv.at[k], a_peer(1))
            send(src, src, a_send.at[k], ar_recv.at[k], a_peer(3))

    def stage_b(k):
        wait(three(k, whole(k)), al_recv.at[k])
        for j in (1, 2, 3):
            src = piece(k, lax.rem(zl + j, 4), lax.rem(ma + 3, 4), half(k, 0))
            send(src, src, b_send.at[k], bl_recv.at[k], a_peer(1))
        wait(three(k, whole(k)), ar_recv.at[k])
        for j in (1, 2, 3):
            src = piece(k, lax.rem(zl + j, 4), lax.rem(ma + 1, 4), half(k, 1))
            send(src, src, b_send.at[k], br_recv.at[k], a_peer(3))

    def stage_c(k):
        wait(three(k, half(k, 0)), bl_recv.at[k])
        wait(three(k, half(k, 1)), br_recv.at[k])
        send(core_half(k, c), core_half(k, c), c_send.at[k], c_recv.at[k], sibling)

    def stage_d(k):
        wait(core_half(k, 0), c_recv.at[k])

    progress = [0]

    def pump(upto):
        while progress[0] < upto:
            t = progress[0]
            if t < NC:
                stage_a(t)
            if 0 <= t - 1 < NC:
                stage_b(t - 1)
            if 0 <= t - 2 < NC:
                stage_c(t - 2)
            progress[0] = t + 1

    def ready(k):
        pump(min(k + 4, NC + 2))
        stage_d(k)

    def norm(v):
        v = v.astype(F32)
        v = v - jnp.mean(v, axis=-1, keepdims=True)
        s = jnp.mean(v * v, axis=-1, keepdims=True)
        return v * lax.rsqrt(s + EPS)

    for copy in local:
        copy.wait()
    nt[...] = norm(xt[...]).astype(BF)

    def share_left(which, value):
        tr[which] = value.T.astype(BF).reshape(8, 2, 64, T)
        cols = pl.ds(pl.multiple_of(c * T, T), T)
        send(tr.at[which, :, oc], lt.at[which, :, :, cols], x_send.at[which], x_recv.at[which], sibling)
        lt[which, :, :, cols] = tr[which, :, c]

    normed_s = norm(xs[...])
    ns[...] = normed_s.astype(BF)
    share_left(0, normed_s)
    pump(2)

    lane = lax.broadcasted_iota(jnp.int32, (1, 128), 1)
    low_f = jnp.where(lane < 64, 1.0, 0.0).astype(F32)
    high_f = 1.0 - low_f
    low_b, high_b = low_f.astype(BF), high_f.astype(BF)

    def softmax_parts(q, k):
        s = mm(q, k, 1, 1) * EXP2_SCALE
        e = jnp.exp2(s - jnp.max(s, axis=-1, keepdims=True))
        return e, 1.0 / jnp.sum(e, axis=-1, keepdims=True)

    def lanes(start):
        return pl.ds(pl.multiple_of(start, 128), 128)

    def teacher_pair(h, carry):
        q, k, v = at[:, lanes(h * 128)], at[:, lanes(DT + h * 128)], at[:, lanes(2 * DT + h * 128)]
        e0, i0 = softmax_parts(q * low_b, k)
        o0 = mm(e0.astype(BF), v) * i0
        e1, i1 = softmax_parts(q * high_b, k)
        o1 = mm(e1.astype(BF), v) * i1
        mt[:, lanes(h * 128)] = (o0 * low_f + o1 * high_f).astype(BF)
        return carry

    def student_pair(h, carry):
        q, k, v = as_[:, lanes(h * 128)], as_[:, lanes(DS + h * 128)], as_[:, lanes(2 * DS + h * 128)]
        e0, i0 = softmax_parts(q * low_b, k)
        p0 = (e0 * i0).astype(BF)
        pr[2 * h] = p0
        o0 = mm(p0, v)
        e1, i1 = softmax_parts(q * high_b, k)
        p1 = (e1 * i1).astype(BF)
        pr[2 * h + 1] = p1
        o1 = mm(p1, v)
        ms[:, lanes(h * 128)] = (o0 * low_f + o1 * high_f).astype(BF)
        return carry

    def weights(k, first, count):
        if CHUNKS[k][0]:
            return Wt[:, :, :, first : first + count].reshape(DT, count)
        return Ws[:, :, :, first : first + count].reshape(DS, count)

    for k in range(6):
        ready(k)
        _, first, count = CHUNKS[k]
        for n in range(first, first + count, 256):
            at[:, n : n + 256] = mm(nt[...], weights(k, n, 256)).astype(BF)
    for part in range(3):
        lax.fori_loop(4 * part, 4 * part + 4, teacher_pair, 0)
        pump(min(progress[0] + 1, NC + 2))
    for k in range(6, 9):
        ready(k)
        _, first, count = CHUNKS[k]
        for n in range(first, first + count, 256):
            as_[:, n : n + 256] = mm(ns[...], weights(k, n, 256)).astype(BF)
    for part in range(2):
        lax.fori_loop(4 * part, 4 * part + 4, student_pair, 0)
        pump(min(progress[0] + 1, NC + 2))
    share_left(1, ms[...].astype(F32))

    for k in (9, 10):
        ready(k)
        _, first, count = CHUNKS[k]
        for n in range(first, first + count, 256):
            cols = slice(n - 4608, n - 4608 + 256)
            xt[:, cols] = (xt[:, cols].astype(F32) + mm(mt[...], weights(k, n, 256))).astype(BF)
    feats = xt[...].astype(F32)
    row = lax.rsqrt(jnp.mean(feats * feats, axis=-1, keepdims=True) + EPS) * DT**-0.5
    along = jnp.broadcast_to(row, (T, 128)).T[0:1, :]
    gt[...] = mm(xt[...], xt[...], 1, 1) * row * along

    ready(11)
    res = xs[...].astype(F32) + mm(ms[...], weights(11, 3072, 1024))
    scale = lax.rsqrt(jnp.mean(res * res, axis=-1, keepdims=True) + EPS) * DS**-0.5
    unit = res * scale
    uh = unit.astype(BF)
    ul = (unit - uh.astype(F32)).astype(BF)
    diff = mm(uh, uh, 1, 1) + (mm(uh, ul, 1, 1) + mm(ul, uh, 1, 1)) - gt[...]
    eh = diff.astype(BF)
    el = (diff - eh.astype(F32)).astype(BF)
    du = 8.0 * (mm(eh, uh) + (mm(eh, ul) + mm(el, uh)))
    og = (scale * (du - jnp.sum(du * unit, axis=-1, keepdims=True) * unit)).astype(BF)
    rg[c, :, 3072:4096] = og
    own_out = rg.at[c, :, 3072:4096]
    send(own_out, own_out, x_send.at[2], x_recv.at[2], sibling)
    for s in range(4):
        for core in range(2):
            mg[:, s * 256 + core * 128 : s * 256 + core * 128 + 128] = mm(
                og, Ws[s, core, :, 3072:4096], 1, 1
            ).astype(BF)

    def backward_pair(h, carry):
        q, k, v = as_[:, lanes(h * 128)], as_[:, lanes(DS + h * 128)], as_[:, lanes(2 * DS + h * 128)]
        up = mg[:, lanes(h * 128)]
        parts = []
        for e, mask in ((0, low_b), (1, high_b)):
            p = pr[2 * h + e]
            pf = p.astype(F32)
            dp = mm(up * mask, v, 1, 1)
            total = jnp.sum(dp * pf, axis=-1, keepdims=True)
            sg = (pf * (dp - total) * 0.125).astype(BF)
            parts.append((mm(sg, k), mm(sg, q, 0, 0), mm(p, up, 0, 0)))
        for i in range(3):
            joined = parts[0][i] * low_f + parts[1][i] * high_f
            rg[c, :, lanes(i * DS + h * 128)] = joined.astype(BF)
        return carry

    lax.fori_loop(0, 8, backward_pair, 0)
    own_in = rg.at[c, :, 0:3072]
    send(own_in, own_in, x_send.at[3], x_recv.at[3], sibling)
    wait(lt.at[0, :, :, 0:T], x_recv.at[0])
    wait(lt.at[1, :, :, 0:T], x_recv.at[1])
    wait(rg.at[0, :, 3072:4096], x_recv.at[2])
    wait(rg.at[0, :, 0:3072], x_recv.at[3])

    def block(a, i):
        return (4 * a + i) * oc + (4 * i + a) * c

    def make(a, i):
        n = block(a, i)
        left = lt[lax.div(n, 12)].reshape(512, 512)
        right = rg[:, :, pl.ds(pl.multiple_of(n * 256, 256), 256)].reshape(512, 256)
        gp[n] = mm(left, right).astype(BF)
        return n

    far, right_a, left_a = lax.rem(ma + 2, 4), lax.rem(ma + 1, 4), lax.rem(ma + 3, 4)

    def far_step(i, carry):
        n = make(far, i)
        send(gp.at[n], l1.at[i], p1_send.at[0, i], pl1_recv.at[i], a_peer(1))
        m = make(far, i + 2)
        send(gp.at[m], r1.at[i], p1_send.at[1, i], pr1_recv.at[i], a_peer(3))
        return carry

    lax.fori_loop(0, 2, far_step, 0)

    def near_step(i, carry):
        n = make(right_a, i + 2)
        send(gp.at[n], l2.at[i + 2], p1_send.at[2, i], pl2_recv.at[i + 2], a_peer(1))
        m = make(left_a, i)
        send(gp.at[m], r2.at[i], p1_send.at[3, i], pr2_recv.at[i], a_peer(3))
        return carry

    lax.fori_loop(0, 2, near_step, 0)

    def sum_make(i, carry):
        make(right_a, i)
        make(left_a, i + 2)
        return carry

    lax.fori_loop(0, 2, sum_make, 0)

    def own_make(i, carry):
        make(ma, i)
        return carry

    lax.fori_loop(0, 4, own_make, 0)

    def sum_step(i, carry):
        n = block(right_a, i)
        wait(l1.at[0], pl1_recv.at[i])
        gp[n] = (gp[n].astype(F32) + l1[i].astype(F32)).astype(BF)
        send(gp.at[n], l2.at[i], p1_send.at[4, i], pl2_recv.at[i], a_peer(1))
        m = block(left_a, i + 2)
        wait(r1.at[0], pr1_recv.at[i])
        gp[m] = (gp[m].astype(F32) + r1[i].astype(F32)).astype(BF)
        send(gp.at[m], r2.at[i + 2], p1_send.at[5, i], pr2_recv.at[i + 2], a_peer(3))
        return carry

    lax.fori_loop(0, 2, sum_step, 0)

    def close(i):
        n = block(ma, i)
        wait(l2.at[0], pl2_recv.at[i])
        wait(r2.at[0], pr2_recv.at[i])
        gp2[i] = (gp[n].astype(F32) + (l2[i].astype(F32) + r2[i].astype(F32))).astype(BF)

    far_b, right_b, left_b = lax.rem(mb + 2, 4), lax.rem(mb + 1, 4), lax.rem(mb + 3, 4)
    upper, lower = slice(0, 256), slice(256, 512)
    close(far_b)
    send(gp2.at[far_b, upper], bl1, p2_send.at[0], ql1_recv, b_peer(1))
    send(gp2.at[far_b, lower], br1, p2_send.at[1], qr1_recv, b_peer(3))
    close(right_b)
    send(gp2.at[right_b, lower], bl2.at[lower], p2_send.at[2], ql2_recv.at[1], b_peer(1))
    close(left_b)
    send(gp2.at[left_b, upper], br2.at[upper], p2_send.at[3], qr2_recv.at[0], b_peer(3))
    close(mb)
    wait(bl1, ql1_recv)
    gp2[right_b, upper] = (gp2[right_b, upper].astype(F32) + bl1[...].astype(F32)).astype(BF)
    send(gp2.at[right_b, upper], bl2.at[upper], p2_send.at[4], ql2_recv.at[0], b_peer(1))
    wait(br1, qr1_recv)
    gp2[left_b, lower] = (gp2[left_b, lower].astype(F32) + br1[...].astype(F32)).astype(BF)
    send(gp2.at[left_b, lower], br2.at[lower], p2_send.at[5], qr2_recv.at[1], b_peer(3))
    for which in range(2):
        wait(bl1, ql2_recv.at[which])
        wait(bl1, qr2_recv.at[which])
    total = gp2[mb].astype(F32) + (bl2[...].astype(F32) + br2[...].astype(F32))
    z3[...] = total.astype(BF).reshape(8, 64, 256)

    for step in range(1, 8):
        send(z3.at[lax.rem(z + step, 8)], zr.at[step - 1], p3_send.at[step - 1], p3_recv.at[step - 1], z_peer(step))
    acc = z3[z].astype(F32)
    for step in range(1, 8):
        wait(zr.at[0], p3_recv.at[step - 1])
        acc = acc + zr[step - 1].astype(F32)
    out[...] = acc

    for k in range(NC):
        wait(three(k, whole(k)), zs_send.at[k])
        wait(six(k, whole(k)), a_send.at[k])
        wait(six(k, half(k, 0)), b_send.at[k])
        wait(core_half(k, 0), c_send.at[k])
    wait(lt.at[0, :, :, 0:T], x_send.at[0])
    wait(lt.at[1, :, :, 0:T], x_send.at[1])
    wait(rg.at[0, :, 3072:4096], x_send.at[2])
    wait(rg.at[0, :, 0:3072], x_send.at[3])
    for which in range(6):
        for i in range(2):
            wait(l1.at[0], p1_send.at[which, i])
        wait(bl1, p2_send.at[which])
    for step in range(7):
        wait(zr.at[0], p3_send.at[step])


def per_device(teacher_tokens, teacher_qkv, teacher_out, student_tokens, student_weights):
    vmem = pltpu.VMEM
    dma = pltpu.SemaphoreType.DMA
    any_spec = pl.BlockSpec(memory_space=pl.ANY)
    return pl.pallas_call(
        kernel,
        out_shape=jax.ShapeDtypeStruct((64, 256), F32),
        in_specs=[any_spec] * 5,
        out_specs=pl.BlockSpec(memory_space=pltpu.VMEM),
        scratch_shapes=[
            vmem((4, 2, RT, TW), BF),
            vmem((4, 2, RS, SW), BF),
            vmem((T, DT), BF),
            vmem((T, DS), BF),
            vmem((T, DT), BF),
            vmem((T, DS), BF),
            vmem((T, 3 * DT), BF),
            vmem((T, DT), BF),
            vmem((T, 3 * DS), BF),
            vmem((16, T, T), BF),
            vmem((T, DS), BF),
            vmem((T, T), F32),
            vmem((2, 8, 2, 64, T), BF),
            vmem((2, 8, 64, 2 * T), BF),
            vmem((2, T, SW), BF),
            vmem((T, DS), BF),
            vmem((16, 512, 256), BF),
            vmem((2, 512, 256), BF),
            vmem((2, 512, 256), BF),
            vmem((4, 512, 256), BF),
            vmem((4, 512, 256), BF),
            vmem((4, 512, 256), BF),
            vmem((256, 256), BF),
            vmem((256, 256), BF),
            vmem((512, 256), BF),
            vmem((512, 256), BF),
            vmem((8, 64, 256), BF),
            vmem((7, 64, 256), BF),
            dma((5,)),
            dma((NC,)), dma((NC,)),
            dma((NC,)), dma((NC,)), dma((NC,)),
            dma((NC,)), dma((NC,)), dma((NC,)),
            dma((NC,)), dma((NC,)),
            dma((4,)), dma((4,)),
            dma((6, 2)), dma((2,)), dma((2,)), dma((4,)), dma((4,)),
            dma((6,)), dma, dma, dma((2,)), dma((2,)),
            dma((7,)), dma((7,)),
        ],
        compiler_params=pltpu.CompilerParams(
            collective_id=0, has_side_effects=True, vmem_limit_bytes=62 * 1024 * 1024
        ),
        cost_estimate=pl.CostEstimate(flops=11_400_000_000, bytes_accessed=30_000_000, transcendentals=2_700_000),
        name="distill",
    )(teacher_tokens, teacher_qkv, teacher_out, student_tokens, student_weights)


def solution(mesh):
    return jax.shard_map(
        per_device,
        mesh=mesh,
        in_specs=(
            P(("rows", "dp"), None),
            P("rows", None),
            P("rows", None),
            P(("rows", "dp"), None),
            P("rows", None),
        ),
        out_specs=P(("group", "rows"), "dp"),
        check_vma=False,
    )
```

time: 1240 us -> 131 us (0.11); the launches traced: 1210 us -> 130 us
  waiting for transfers between devices: 1100 us -> 0 us
  Pallas kernels: 0 us -> 128 us
  local copies, waits for them, and re-layouts: 39.7 us -> 1.47 us
  matrix products: 34.8 us -> 0 us
  other arithmetic: 22.3 us -> 0 us
  between operations: 13.5 us -> 0.01 us
    reduce_scatter x1 -> x0, waiting for transfers between devices: 811 us -> none  [per_device(): lax.psum_scatter(local_terms, ('rows', 'dp'), scatter_dimension=0, tiled=...]
    all_gather x3 -> x0, waiting for transfers between devices: 276 us -> none  [the longest x1 150 us: per_device(): shard_rows = lax.all_gather(teacher_qkv, 'rows', axis=0, tiled=True)]
    pallas_call x0 -> x1, Pallas kernels: none -> 128 us  [per_device(): pl.pallas_call(kernel, out_shape=jax.ShapeDtypeStruct((64, 256), F32), in...]
    dot_general x4 -> x0, matrix products: 34.8 us -> none  [the longest x1 14.1 us: product(): return jnp.dot(normed_t, shard_rows, preferred_element_type=jnp.float32)]
    sub x1 -> x0, other arithmetic: 15.9 us -> none  [attention_fwd(): scores = scores - jnp.max(scores, axis=-1, keepdims=True)]
    reshape x1 -> x0, local copies, waits for them, and re-layouts: 12.6 us -> none  [attention_fwd(): shaped = qkv_act.reshape(images, IMG_TOK, 3, head_count, head_size)]
  transfers between devices with their start and end apart: 6 -> 0, of which waited for: 4 -> 0; matrix products, arithmetic and copies ran while one was open for 7% -> 0% of each run, Pallas kernels for 0% -> 0%
where the time goes in v1:
time: 131 us; the launch traced here: 130 us
  Pallas kernels  128 us (98%)
  local copies, waits for them, and re-layouts  1.47 us (1%)
    pallas_call x1, Pallas kernels, per_device(): pl.pallas_call(kernel, out_shape=jax.ShapeDtypeStruct((64, 256), F32), in...  128 us

profile of v1, /device:TPU:4, one launch (start us, length us, event | category | flops | bytes accessed | tf_op | source)
XLA Modules:
  0.0 129.9 jit_solution(1946513469678279793)
XLA Ops:
  0.0 128.4 %distill.1 = f32[64,256]{1,0:T(8,128)} custom-call(bf16[512,1536]{1,0:T(8,128)(2,1)} %tt.1, bf16[192,4608]{1,0:T(8,128)(2,1)} %tq.1, bf16[192,1536]{1,0:T(8,128)(2,1)} %to.1, bf16[512,1024]{1,0:T(8,128)(2,1)} %st.1, bf16[128,4096]{1,0:T(8,128)(2,1)} %sw.1), custom_call_target="tpu_custom_call" | custom-call | flops 11399999488 | bytes 30000000 | tf_op jit(solution)/shard_map/distill/pallas_call | solution.py:420
  128.4 1.5 %copy.7 = f32[64,256]{1,0:T(8,128)} copy(f32[64,256]{1,0:T(8,128)} %distill.1) | data formatting | bytes 131072

commit v2 on v1

--- a/solution.py
+++ b/solution.py
@@ -22,10 +22,10 @@
 EXP2_SCALE = 0.125 * 1.4426950408889634
 
 CHUNKS = (
-    [(True, 768 * i, 768) for i in range(6)]
-    + [(False, 1024 * i, 1024) for i in range(3)]
-    + [(True, 4608 + 768 * i, 768) for i in range(2)]
-    + [(False, 3072, 1024)]
+    [(True, 0, 256), (True, 256, 512)]
+    + [(True, 768 * i, 768) for i in range(1, 6)]
+    + [(False, 1024 * i, 1024) for i in range(4)]
+    + [(True, 4608, 768), (True, 5376, 512), (True, 5888, 256)]
 )
 NC = len(CHUNKS)
 
@@ -36,10 +36,10 @@
 
 def kernel(
     tt, tq, to, st, sw, out,
-    Wt, Ws, xt, xs, nt, ns, at, mt, as_, pr, ms, gt, tr, lt, rg, mg,
-    gp, l1, r1, l2, r2, gp2, bl1, br1, bl2, br2, z3, zr,
+    Wt, Ws, xt, xs, nt, ns, at, mt, as_, ex, iv, ms, rs, uh_ref, ul_ref, gs, gt, tr, lt, rg,
+    gp, rx, gp2, bl1, br1, bl2, br2, z3, zr,
     loc_sem, zs_send, zs_recv, a_send, al_recv, ar_recv, b_send, bl_recv, br_recv, c_send, c_recv,
-    x_send, x_recv, p1_send, pl1_recv, pr1_recv, pl2_recv, pr2_recv,
+    x_send, x_recv, g_send, g_recv, p1_send, p1_recv,
     p2_send, ql1_recv, qr1_recv, ql2_recv, qr2_recv, p3_send, p3_recv,
 ):
     g = lax.axis_index("group")
@@ -87,6 +87,21 @@
     peers = [z_peer(s) for s in range(1, 8)] + [a_peer(1), a_peer(3), b_peer(1), b_peer(3), sibling]
     for peer in peers:
         pl.semaphore_signal(barrier, inc=1, device_id=peer, device_id_type=MESH)
+
+    def norm(v):
+        v = v.astype(F32)
+        v = v - jnp.mean(v, axis=-1, keepdims=True)
+        s = jnp.mean(v * v, axis=-1, keepdims=True)
+        return v * lax.rsqrt(s + EPS)
+
+    local[0].wait()
+    nt[...] = norm(xt[...]).astype(BF)
+    local[1].wait()
+    normed_s = norm(xs[...])
+    ns[...] = normed_s.astype(BF)
+    tr[0] = normed_s.T.astype(BF).reshape(8, 2, 64, T)
+    for copy in local[2:]:
+        copy.wait()
     pl.semaphore_wait(barrier, len(peers))
 
     def piece(chunk, shard, quarter, cols):
@@ -170,201 +185,228 @@
         pump(min(k + 4, NC + 2))
         stage_d(k)
 
-    def norm(v):
-        v = v.astype(F32)
-        v = v - jnp.mean(v, axis=-1, keepdims=True)
-        s = jnp.mean(v * v, axis=-1, keepdims=True)
-        return v * lax.rsqrt(s + EPS)
-
-    for copy in local:
-        copy.wait()
-    nt[...] = norm(xt[...]).astype(BF)
-
-    def share_left(which, value):
-        tr[which] = value.T.astype(BF).reshape(8, 2, 64, T)
+    def share_left(which):
         cols = pl.ds(pl.multiple_of(c * T, T), T)
         send(tr.at[which, :, oc], lt.at[which, :, :, cols], x_send.at[which], x_recv.at[which], sibling)
         lt[which, :, :, cols] = tr[which, :, c]
 
-    normed_s = norm(xs[...])
-    ns[...] = normed_s.astype(BF)
-    share_left(0, normed_s)
-    pump(2)
+    pump(1)
+    share_left(0)
 
     lane = lax.broadcasted_iota(jnp.int32, (1, 128), 1)
     low_f = jnp.where(lane < 64, 1.0, 0.0).astype(F32)
     high_f = 1.0 - low_f
     low_b, high_b = low_f.astype(BF), high_f.astype(BF)
-
-    def softmax_parts(q, k):
-        s = mm(q, k, 1, 1) * EXP2_SCALE
-        e = jnp.exp2(s - jnp.max(s, axis=-1, keepdims=True))
-        return e, 1.0 / jnp.sum(e, axis=-1, keepdims=True)
-
-    def lanes(start):
-        return pl.ds(pl.multiple_of(start, 128), 128)
-
-    def teacher_pair(h, carry):
+    zero_b = jnp.zeros((T, 128), BF)
+
+    def lanes(start, count=128):
+        return pl.ds(pl.multiple_of(start, 128), count)
+
+    def both(v):
+        return jnp.concatenate([v * low_b, v * high_b], axis=0)
+
+    def attend(q, k, v):
+        s = mm(both(q), k, 1, 1)
+        e = jnp.exp2((s - jnp.max(s, axis=-1, keepdims=True)) * EXP2_SCALE).astype(BF)
+        e0, e1 = e[:T], e[T:]
+        ones = jnp.concatenate([zero_b + low_b, zero_b + high_b], axis=0)
+        right = jnp.concatenate([both(v), ones], axis=1)
+        joined = mm(jnp.concatenate([e0, e1], axis=1), right)
+        inv = 1.0 / joined[:, 128:]
+        return e0, e1, joined[:, :128] * inv, inv
+
+    def teacher_pair(h):
         q, k, v = at[:, lanes(h * 128)], at[:, lanes(DT + h * 128)], at[:, lanes(2 * DT + h * 128)]
-        e0, i0 = softmax_parts(q * low_b, k)
-        o0 = mm(e0.astype(BF), v) * i0
-        e1, i1 = softmax_parts(q * high_b, k)
-        o1 = mm(e1.astype(BF), v) * i1
-        mt[:, lanes(h * 128)] = (o0 * low_f + o1 * high_f).astype(BF)
-        return carry
-
-    def student_pair(h, carry):
+        mt[:, lanes(h * 128)] = attend(q, k, v)[2].astype(BF)
+
+    def student_pair(h):
         q, k, v = as_[:, lanes(h * 128)], as_[:, lanes(DS + h * 128)], as_[:, lanes(2 * DS + h * 128)]
-        e0, i0 = softmax_parts(q * low_b, k)
-        p0 = (e0 * i0).astype(BF)
-        pr[2 * h] = p0
-        o0 = mm(p0, v)
-        e1, i1 = softmax_parts(q * high_b, k)
-        p1 = (e1 * i1).astype(BF)
-        pr[2 * h + 1] = p1
-        o1 = mm(p1, v)
-        ms[:, lanes(h * 128)] = (o0 * low_f + o1 * high_f).astype(BF)
-        return carry
+        e0, e1, mixed, inv = attend(q, k, v)
+        ex[h, 0:T] = e0
+        ex[h, T : 2 * T] = e1
+        iv[:, lanes(h * 128)] = inv
+        ms[:, lanes(h * 128)] = mixed.astype(BF)
+
+    def pairs(fn, first, last):
+        def two(i, carry):
+            fn(2 * i)
+            fn(2 * i + 1)
+            return carry
+
+        lax.fori_loop(first // 2, last // 2, two, 0)
 
     def weights(k, first, count):
         if CHUNKS[k][0]:
             return Wt[:, :, :, first : first + count].reshape(DT, count)
         return Ws[:, :, :, first : first + count].reshape(DS, count)
 
-    for k in range(6):
+    for k in range(7):
         ready(k)
         _, first, count = CHUNKS[k]
         for n in range(first, first + count, 256):
             at[:, n : n + 256] = mm(nt[...], weights(k, n, 256)).astype(BF)
     for part in range(3):
-        lax.fori_loop(4 * part, 4 * part + 4, teacher_pair, 0)
+        pairs(teacher_pair, 4 * part, 4 * part + 4)
         pump(min(progress[0] + 1, NC + 2))
-    for k in range(6, 9):
+    for k in range(7, 10):
         ready(k)
         _, first, count = CHUNKS[k]
         for n in range(first, first + count, 256):
             as_[:, n : n + 256] = mm(ns[...], weights(k, n, 256)).astype(BF)
     for part in range(2):
-        lax.fori_loop(4 * part, 4 * part + 4, student_pair, 0)
+        pairs(student_pair, 4 * part, 4 * part + 4)
         pump(min(progress[0] + 1, NC + 2))
-    share_left(1, ms[...].astype(F32))
-
-    for k in (9, 10):
+    tr[1] = ms[...].astype(F32).T.astype(BF).reshape(8, 2, 64, T)
+    share_left(1)
+
+    ready(10)
+    square = jnp.zeros((T, 1), F32)
+    for n in range(0, DS, 256):
+        res = xs[:, n : n + 256].astype(F32) + mm(ms[...], weights(10, 3072 + n, 256))
+        square += jnp.sum(res * res, axis=-1, keepdims=True)
+        rs[:, n : n + 256] = res
+    scale = lax.rsqrt(square / DS + EPS) * DS**-0.5
+    for n in range(0, DS, 256):
+        unit = rs[:, n : n + 256] * scale
+        rs[:, n : n + 256] = unit
+        high = unit.astype(BF)
+        uh_ref[:, n : n + 256] = high
+        ul_ref[:, n : n + 256] = (unit - high.astype(F32)).astype(BF)
+    cross = mm(uh_ref[...], ul_ref[...], 1, 1)
+    gs[...] = mm(uh_ref[...], uh_ref[...], 1, 1) + (cross + cross.T)
+
+    square = jnp.zeros((T, 1), F32)
+    for k in (11, 12, 13):
         ready(k)
         _, first, count = CHUNKS[k]
         for n in range(first, first + count, 256):
             cols = slice(n - 4608, n - 4608 + 256)
-            xt[:, cols] = (xt[:, cols].astype(F32) + mm(mt[...], weights(k, n, 256))).astype(BF)
-    feats = xt[...].astype(F32)
-    row = lax.rsqrt(jnp.mean(feats * feats, axis=-1, keepdims=True) + EPS) * DT**-0.5
+            feats = (xt[:, cols].astype(F32) + mm(mt[...], weights(k, n, 256))).astype(BF)
+            wide = feats.astype(F32)
+            square += jnp.sum(wide * wide, axis=-1, keepdims=True)
+            term = mm(feats, feats, 1, 1)
+            if n == 4608:
+                gt[...] = term
+            else:
+                gt[...] += term
+    row = lax.rsqrt(square / DT + EPS) * DT**-0.5
     along = jnp.broadcast_to(row, (T, 128)).T[0:1, :]
-    gt[...] = mm(xt[...], xt[...], 1, 1) * row * along
-
-    ready(11)
-    res = xs[...].astype(F32) + mm(ms[...], weights(11, 3072, 1024))
-    scale = lax.rsqrt(jnp.mean(res * res, axis=-1, keepdims=True) + EPS) * DS**-0.5
-    unit = res * scale
-    uh = unit.astype(BF)
-    ul = (unit - uh.astype(F32)).astype(BF)
-    diff = mm(uh, uh, 1, 1) + (mm(uh, ul, 1, 1) + mm(ul, uh, 1, 1)) - gt[...]
+    diff = 8.0 * (gs[...] - gt[...] * row * along)
+
     eh = diff.astype(BF)
     el = (diff - eh.astype(F32)).astype(BF)
-    du = 8.0 * (mm(eh, uh) + (mm(eh, ul) + mm(el, uh)))
-    og = (scale * (du - jnp.sum(du * unit, axis=-1, keepdims=True) * unit)).astype(BF)
-    rg[c, :, 3072:4096] = og
+    du = mm(eh, uh_ref[...]) + mm(jnp.concatenate([eh, el], axis=1), jnp.concatenate([ul_ref[...], uh_ref[...]], axis=0))
+    unit = rs[...]
+    rg[c, :, 3072:4096] = (scale * (du - jnp.sum(du * unit, axis=-1, keepdims=True) * unit)).astype(BF)
     own_out = rg.at[c, :, 3072:4096]
     send(own_out, own_out, x_send.at[2], x_recv.at[2], sibling)
-    for s in range(4):
-        for core in range(2):
-            mg[:, s * 256 + core * 128 : s * 256 + core * 128 + 128] = mm(
-                og, Ws[s, core, :, 3072:4096], 1, 1
-            ).astype(BF)
-
-    def backward_pair(h, carry):
-        q, k, v = as_[:, lanes(h * 128)], as_[:, lanes(DS + h * 128)], as_[:, lanes(2 * DS + h * 128)]
-        up = mg[:, lanes(h * 128)]
-        parts = []
-        for e, mask in ((0, low_b), (1, high_b)):
-            p = pr[2 * h + e]
-            pf = p.astype(F32)
-            dp = mm(up * mask, v, 1, 1)
-            total = jnp.sum(dp * pf, axis=-1, keepdims=True)
-            sg = (pf * (dp - total) * 0.125).astype(BF)
-            parts.append((mm(sg, k), mm(sg, q, 0, 0), mm(p, up, 0, 0)))
-        for i in range(3):
-            joined = parts[0][i] * low_f + parts[1][i] * high_f
-            rg[c, :, lanes(i * DS + h * 128)] = joined.astype(BF)
-        return carry
-
-    lax.fori_loop(0, 8, backward_pair, 0)
-    own_in = rg.at[c, :, 0:3072]
-    send(own_in, own_in, x_send.at[3], x_recv.at[3], sibling)
+
+    def where_to(section, group):
+        i = group * oc + section * c
+        return lax.rem(section * oc + group * c - ma + 4, 4), i
+
+    def transfer(n, direction, slot):
+        send(
+            gp.at[n], rx.at[direction, slot], p1_send.at[n], p1_recv.at[direction, slot], a_peer(1 + 2 * direction)
+        )
+
+    def emit(section, group):
+        n = 4 * section + group
+        left = lt[section // 3].reshape(512, 512)
+        right = rg[:, :, pl.ds(pl.multiple_of(n * 256, 256), 256)].reshape(512, 256)
+        gp[n] = mm(left, right).astype(BF)
+        rel, i = where_to(section, group)
+        upper = lax.div(i, 2)
+
+        @pl.when(rel == 2)
+        def _():
+            transfer(n, upper, i - 2 * upper)
+
+        @pl.when((rel == 1) & (i >= 2) | (rel == 3) & (i < 2))
+        def _():
+            transfer(n, lax.div(rel, 2), 2 + i)
+
+    def settle(section, group):
+        n = 4 * section + group
+        rel, i = where_to(section, group)
+        direction = lax.div(rel, 2)
+
+        @pl.when((rel == 1) & (i < 2) | (rel == 3) & (i >= 2))
+        def _():
+            slot = i - 2 * direction
+            wait(rx.at[0, 0], p1_recv.at[direction, slot])
+            gp[n] = (gp[n].astype(F32) + rx[direction, slot].astype(F32)).astype(BF)
+            transfer(n, direction, 2 + i)
+
+    def own_cols(core, group):
+        return rg.at[core, :, lanes(group * 256, 256)], rg.at[core, :, lanes(DS + group * 256, 256)], rg.at[
+            core, :, lanes(2 * DS + group * 256, 256)
+        ]
+
+    ones = zero_b + 1.0
+
+    def backward(group):
+        first = group * 256
+        og = rg[c, :, 3072:4096]
+        up = mm(og, Ws[group, :, :, 3072:4096].reshape(256, DS), 1, 1)
+        up = up * iv[:, lanes(first, 256)]
+        rows = up * ms[:, lanes(first, 256)].astype(F32) * -0.125
+        for p in range(2):
+            at0 = first + 128 * p
+            q, k, v = as_[:, lanes(at0)], as_[:, lanes(DS + at0)], as_[:, lanes(2 * DS + at0)]
+            u = up[:, 128 * p : 128 * p + 128]
+            grads = both(u.astype(BF))
+            left = jnp.concatenate([both((u * 0.125).astype(BF)), both(rows[:, 128 * p : 128 * p + 128].astype(BF))], axis=1)
+            dp = mm(left, jnp.concatenate([v, ones], axis=1), 1, 1)
+            e = ex[2 * group + p]
+            sg = (e.astype(F32) * dp).astype(BF)
+            wide = jnp.concatenate([sg[:T], sg[T:]], axis=1)
+            rg[c, :, lanes(at0)] = mm(wide, both(k)).astype(BF)
+            rg[c, :, lanes(DS + at0)] = mm(sg, both(q), 0, 0).astype(BF)
+            rg[c, :, lanes(2 * DS + at0)] = mm(e, grads, 0, 0).astype(BF)
+        for section, mine in enumerate(own_cols(c, group)):
+            send(mine, mine, g_send.at[group, section], g_recv.at[group, section], sibling)
+
+    def terms(group):
+        for section, theirs in enumerate(own_cols(oc, group)):
+            wait(theirs, g_recv.at[group, section])
+            emit(section, group)
+
+    def nth(k):
+        return lax.rem(y + 2 + lax.div(k * (k + 1), 2), 4)
+
+    first_group = lax.rem(y + 2, 4)
+    backward(first_group)
     wait(lt.at[0, :, :, 0:T], x_recv.at[0])
     wait(lt.at[1, :, :, 0:T], x_recv.at[1])
     wait(rg.at[0, :, 3072:4096], x_recv.at[2])
-    wait(rg.at[0, :, 0:3072], x_recv.at[3])
-
-    def block(a, i):
-        return (4 * a + i) * oc + (4 * i + a) * c
-
-    def make(a, i):
-        n = block(a, i)
-        left = lt[lax.div(n, 12)].reshape(512, 512)
-        right = rg[:, :, pl.ds(pl.multiple_of(n * 256, 256), 256)].reshape(512, 256)
-        gp[n] = mm(left, right).astype(BF)
-        return n
-
-    far, right_a, left_a = lax.rem(ma + 2, 4), lax.rem(ma + 1, 4), lax.rem(ma + 3, 4)
-
-    def far_step(i, carry):
-        n = make(far, i)
-        send(gp.at[n], l1.at[i], p1_send.at[0, i], pl1_recv.at[i], a_peer(1))
-        m = make(far, i + 2)
-        send(gp.at[m], r1.at[i], p1_send.at[1, i], pr1_recv.at[i], a_peer(3))
+
+    def emit_out(k, carry):
+        emit(3, nth(k))
         return carry
 
-    lax.fori_loop(0, 2, far_step, 0)
-
-    def near_step(i, carry):
-        n = make(right_a, i + 2)
-        send(gp.at[n], l2.at[i + 2], p1_send.at[2, i], pl2_recv.at[i + 2], a_peer(1))
-        m = make(left_a, i)
-        send(gp.at[m], r2.at[i], p1_send.at[3, i], pr2_recv.at[i], a_peer(3))
+    lax.fori_loop(0, 4, emit_out, 0)
+    terms(first_group)
+
+    def later(k, carry):
+        backward(nth(k))
+        terms(nth(k))
         return carry
 
-    lax.fori_loop(0, 2, near_step, 0)
-
-    def sum_make(i, carry):
-        make(right_a, i)
-        make(left_a, i + 2)
+    lax.fori_loop(1, 4, later, 0)
+
+    def settle_group(k, carry):
+        for section in (3, 0, 1, 2):
+            settle(section, nth(k))
         return carry
 
-    lax.fori_loop(0, 2, sum_make, 0)
-
-    def own_make(i, carry):
-        make(ma, i)
-        return carry
-
-    lax.fori_loop(0, 4, own_make, 0)
-
-    def sum_step(i, carry):
-        n = block(right_a, i)
-        wait(l1.at[0], pl1_recv.at[i])
-        gp[n] = (gp[n].astype(F32) + l1[i].astype(F32)).astype(BF)
-        send(gp.at[n], l2.at[i], p1_send.at[4, i], pl2_recv.at[i], a_peer(1))
-        m = block(left_a, i + 2)
-        wait(r1.at[0], pr1_recv.at[i])
-        gp[m] = (gp[m].astype(F32) + r1[i].astype(F32)).astype(BF)
-        send(gp.at[m], r2.at[i + 2], p1_send.at[5, i], pr2_recv.at[i + 2], a_peer(3))
-        return carry
-
-    lax.fori_loop(0, 2, sum_step, 0)
+    lax.fori_loop(0, 4, settle_group, 0)
 
     def close(i):
-        n = block(ma, i)
-        wait(l2.at[0], pl2_recv.at[i])
-        wait(r2.at[0], pr2_recv.at[i])
-        gp2[i] = (gp[n].astype(F32) + (l2[i].astype(F32) + r2[i].astype(F32))).astype(BF)
+        n = (4 * ma + i) * oc + (4 * i + ma) * c
+        wait(rx.at[0, 0], p1_recv.at[0, 2 + i])
+        wait(rx.at[0, 0], p1_recv.at[1, 2 + i])
+        gp2[i] = (gp[n].astype(F32) + (rx[0, 2 + i].astype(F32) + rx[1, 2 + i].astype(F32))).astype(BF)
 
     far_b, right_b, left_b = lax.rem(mb + 2, 4), lax.rem(mb + 1, 4), lax.rem(mb + 3, 4)
     upper, lower = slice(0, 256), slice(256, 512)
@@ -404,10 +446,21 @@
     wait(lt.at[0, :, :, 0:T], x_send.at[0])
     wait(lt.at[1, :, :, 0:T], x_send.at[1])
     wait(rg.at[0, :, 3072:4096], x_send.at[2])
-    wait(rg.at[0, :, 0:3072], x_send.at[3])
+    for group in range(4):
+        for section, mine in enumerate(own_cols(0, group)):
+            wait(mine, g_send.at[group, section])
+
+    def sent(n, carry):
+        rel, _ = where_to(lax.div(n, 4), lax.rem(n, 4))
+
+        @pl.when(rel != 0)
+        def _():
+            wait(rx.at[0, 0], p1_send.at[n])
+
+        return carry
+
+    lax.fori_loop(0, 16, sent, 0)
     for which in range(6):
-        for i in range(2):
-            wait(l1.at[0], p1_send.at[which, i])
         wait(bl1, p2_send.at[which])
     for step in range(7):
         wait(zr.at[0], p3_send.at[step])
@@ -432,18 +485,19 @@
             vmem((T, 3 * DT), BF),
             vmem((T, DT), BF),
             vmem((T, 3 * DS), BF),
-            vmem((16, T, T), BF),
+            vmem((8, 2 * T, T), BF),
+            vmem((T, DS), F32),
             vmem((T, DS), BF),
+            vmem((T, DS), F32),
+            vmem((T, DS), BF),
+            vmem((T, DS), BF),
+            vmem((T, T), F32),
             vmem((T, T), F32),
             vmem((2, 8, 2, 64, T), BF),
             vmem((2, 8, 64, 2 * T), BF),
             vmem((2, T, SW), BF),
-            vmem((T, DS), BF),
             vmem((16, 512, 256), BF),
-            vmem((2, 512, 256), BF),
-            vmem((2, 512, 256), BF),
-            vmem((4, 512, 256), BF),
-            vmem((4, 512, 256), BF),
+            vmem((2, 6, 512, 256), BF),
             vmem((4, 512, 256), BF),
             vmem((256, 256), BF),
             vmem((256, 256), BF),
@@ -456,8 +510,9 @@
             dma((NC,)), dma((NC,)), dma((NC,)),
             dma((NC,)), dma((NC,)), dma((NC,)),
             dma((NC,)), dma((NC,)),
-            dma((4,)), dma((4,)),
-            dma((6, 2)), dma((2,)), dma((2,)), dma((4,)), dma((4,)),
+            dma((3,)), dma((3,)),
+            dma((4, 3)), dma((4, 3)),
+            dma((16,)), dma((2, 6)),
             dma((6,)), dma, dma, dma((2,)), dma((2,)),
             dma((7,)), dma((7,)),
         ],

time: 131 us -> 121 us (0.924)
  Pallas kernels: 128 us -> 119 us
    pallas_call x1, Pallas kernels: 128 us -> 119 us  [per_device(): pl.pallas_call(kernel, out_shape=jax.ShapeDtypeStruct((64, 256), F32), in...]
where the time goes in v2:
time: 121 us
  Pallas kernels  119 us (98%)
  local copies, waits for them, and re-layouts  1.47 us (1%)
    pallas_call x1, Pallas kernels, per_device(): pl.pallas_call(kernel, out_shape=jax.ShapeDtypeStruct((64, 256), F32), in...  119 us

profile of v2, /device:TPU:4, one launch (start us, length us, event | category | flops | bytes accessed | tf_op | source)
XLA Modules:
  0.0 120.7 jit_solution(597345198737706431)
XLA Ops:
  0.0 119.2 %distill.1 = f32[64,256]{1,0:T(8,128)} custom-call(bf16[512,1536]{1,0:T(8,128)(2,1)} %tt.1, bf16[192,4608]{1,0:T(8,128)(2,1)} %tq.1, bf16[192,1536]{1,0:T(8,128)(2,1)} %to.1, bf16[512,1024]{1,0:T(8,128)(2,1)} %st.1, bf16[128,4096]{1,0:T(8,128)(2,1)} %sw.1), custom_call_target="tpu_custom_call" | custom-call | flops 11399999488 | bytes 30000000 | tf_op jit(solution)/shard_map/distill/pallas_call | solution.py:473
  119.2 1.5 %copy.7 = f32[64,256]{1,0:T(8,128)} copy(f32[64,256]{1,0:T(8,128)} %distill.1) | data formatting | bytes 131072

commit v3 on v2

--- a/solution.py
+++ b/solution.py
@@ -1,3 +1,5 @@
+import functools
+
 import jax
 import jax.numpy as jnp
 from jax import lax
@@ -22,12 +24,60 @@
 EXP2_SCALE = 0.125 * 1.4426950408889634
 
 CHUNKS = (
-    [(True, 0, 256), (True, 256, 512)]
-    + [(True, 768 * i, 768) for i in range(1, 6)]
-    + [(False, 1024 * i, 1024) for i in range(4)]
-    + [(True, 4608, 768), (True, 5376, 512), (True, 5888, 256)]
+    [(True, 0, 256, True), (True, 256, 512, True)]
+    + [(True, 768 * i, 768, True) for i in range(1, 6)]
+    + [(False, 1024 * i, 1024, True) for i in range(4)]
+    + [(True, 4608, 768, True), (True, 5376, 512, False), (True, 5888, 256, False)]
 )
 NC = len(CHUNKS)
+
+
+WINDOW = 3
+SLACK = 0.0
+Z_RATE, RING_RATE, CORE_RATE, HOP = 85e3, 80e3, 500e3, 1.5
+
+
+def plan(tasks):
+    z_free, ring_free, core_free = 0.0, 0.0, 0.0
+    events, pending = [], [(0.0, 0, k) for k in range(WINDOW)]
+    while pending:
+        pending.sort()
+        when, stage, k = pending.pop(0)
+        teacher, _, count, ring = CHUNKS[k]
+        size = (RT if teacher else RS) * count * 2
+        if stage == 0:
+            z_free = max(z_free, when) + 2 * (size // 4 if ring else size) / Z_RATE
+            events.append((z_free + HOP, 1, k))
+            pending.append((z_free + HOP, 1, k))
+            if k + WINDOW < NC:
+                pending.append((z_free + HOP, 0, k + WINDOW))
+        elif stage == 1:
+            z_free = max(z_free, when) + (size // 4 if ring else size) / Z_RATE
+            events.append((z_free + HOP, 2, k))
+            pending.append((z_free + HOP, 2 if ring else 4, k))
+        elif stage == 2:
+            ring_free = max(ring_free, when) + 0.75 * size / RING_RATE
+            events.append((ring_free + HOP, 3, k))
+            pending.append((ring_free + HOP, 3, k))
+        elif stage == 3:
+            ring_free = max(ring_free, when) + 0.375 * size / RING_RATE
+            pending.append((ring_free + HOP, 4, k))
+        else:
+            events.append((when, 4, k))
+            core_free = max(core_free, when) + 4 * size / CORE_RATE
+            events.append((core_free + HOP, 5, k))
+    events.sort()
+    order, clock, ready = [], 0.0, set()
+    for index, (need, cost) in enumerate(tasks):
+        while events and (events[0][0] <= clock + cost - SLACK or (need is not None and need not in ready)):
+            when, stage, k = events.pop(0)
+            clock = max(clock, when)
+            order.append((stage, k))
+            if stage == 5:
+                ready.add(k)
+        order.append((0, index))
+        clock += cost
+    return order
 
 
 def mm(a, b, ca=1, cb=0):
@@ -38,7 +88,8 @@
     tt, tq, to, st, sw, out,
     Wt, Ws, xt, xs, nt, ns, at, mt, as_, ex, iv, ms, rs, uh_ref, ul_ref, gs, gt, tr, lt, rg,
     gp, rx, gp2, bl1, br1, bl2, br2, z3, zr,
-    loc_sem, zs_send, zs_recv, a_send, al_recv, ar_recv, b_send, bl_recv, br_recv, c_send, c_recv,
+    loc_sem, z_send, zl_recv, zr_recv, z2_send, zf_recv, zg_recv,
+    a_send, al_recv, ar_recv, b_send, bl_recv, br_recv, c_send, c_recv,
     x_send, x_recv, g_send, g_recv, p1_send, p1_recv,
     p2_send, ql1_recv, qr1_recv, ql2_recv, qr2_recv, p3_send, p3_recv,
 ):
@@ -104,93 +155,101 @@
         copy.wait()
     pl.semaphore_wait(barrier, len(peers))
 
-    def piece(chunk, shard, quarter, cols):
-        teacher = CHUNKS[chunk][0]
-        size = QT if teacher else QS
-        rows = pl.ds(pl.multiple_of(quarter * size, 16), size)
-        return (Wt if teacher else Ws).at[shard, c, rows, cols]
-
-    def whole(chunk):
-        _, first, count = CHUNKS[chunk]
-        return slice(first, first + count)
-
-    def half(chunk, which):
-        _, first, count = CHUNKS[chunk]
+    def size_of(k):
+        teacher, _, _, ring = CHUNKS[k]
+        full = RT if teacher else RS
+        return full // 4 if ring else full
+
+    def buffer(k):
+        return Wt if CHUNKS[k][0] else Ws
+
+    def piece(k, shard, quarter, cols):
+        size = size_of(k)
+        rows = pl.ds(pl.multiple_of(quarter * size, 16), size) if CHUNKS[k][3] else slice(0, size)
+        return buffer(k).at[shard, c, rows, cols]
+
+    def part(k, which=None):
+        _, first, count, _ = CHUNKS[k]
+        if which is None:
+            return slice(first, first + count)
         return slice(first + which * count // 2, first + (which + 1) * count // 2)
 
-    def three(chunk, cols):
-        teacher = CHUNKS[chunk][0]
-        return (Wt.at[0, 0, 0 : 3 * QT, cols]) if teacher else (Ws.at[0, 0, 0 : 3 * QS, cols])
-
-    def six(chunk, cols):
-        teacher = CHUNKS[chunk][0]
-        return (Wt.at[0, :, 0 : 3 * QT, cols]) if teacher else (Ws.at[0, :, 0 : 3 * QS, cols])
-
-    def core_half(chunk, core):
-        teacher = CHUNKS[chunk][0]
-        return (Wt if teacher else Ws).at[:, core, :, whole(chunk)]
-
-    for k in range(NC):
-        teacher, first, count = CHUNKS[k]
-        size = QT if teacher else QS
-        rows = pl.ds(pl.multiple_of(ma * size, 16), size)
+    def some(k, pieces, cols):
+        rows = pieces * size_of(k)
+        full = RT if CHUNKS[k][0] else RS
+        if rows <= full:
+            return buffer(k).at[0, 0, 0:rows, cols]
+        if rows == pieces * full:
+            return buffer(k).at[0:pieces, 0, :, cols]
+        return buffer(k).at[0, :, 0 : rows // 2, cols]
+
+    def core_half(k, core):
+        return buffer(k).at[:, core, :, part(k)]
+
+    up_z, down_z = lax.rem(zl + 1, 4), lax.rem(zl + 3, 4)
+    opposite = lax.rem(zl + 2, 4)
+
+    def stage_0(k):
+        teacher, first, count, ring = CHUNKS[k]
+        size = size_of(k)
+        rows = pl.ds(pl.multiple_of(ma * size, 16), size) if ring else slice(0, size)
         if not teacher:
-            src = sw.at[rows, whole(k)]
+            src = sw.at[rows, part(k)]
         elif first < 4608:
-            src = tq.at[rows, whole(k)]
+            src = tq.at[rows, part(k)]
         else:
             src = to.at[rows, slice(first - 4608, first - 4608 + count)]
-        for step in (1, 7, 2 if k % 2 == 0 else 6):
-            send(src, piece(k, zl, ma, whole(k)), zs_send.at[k], zs_recv.at[k], z_peer(step))
-
-    def stage_a(k):
-        wait(three(k, whole(k)), zs_recv.at[k])
-        for j in (1, 2, 3):
-            src = piece(k, lax.rem(zl + j, 4), ma, whole(k))
-            send(src, src, a_send.at[k], al_recv.at[k], a_peer(1))
-            send(src, src, a_send.at[k], ar_recv.at[k], a_peer(3))
-
-    def stage_b(k):
-        wait(three(k, whole(k)), al_recv.at[k])
-        for j in (1, 2, 3):
-            src = piece(k, lax.rem(zl + j, 4), lax.rem(ma + 3, 4), half(k, 0))
-            send(src, src, b_send.at[k], bl_recv.at[k], a_peer(1))
-        wait(three(k, whole(k)), ar_recv.at[k])
-        for j in (1, 2, 3):
-            src = piece(k, lax.rem(zl + j, 4), lax.rem(ma + 1, 4), half(k, 1))
-            send(src, src, b_send.at[k], br_recv.at[k], a_peer(3))
-
-    def stage_c(k):
-        wait(three(k, half(k, 0)), bl_recv.at[k])
-        wait(three(k, half(k, 1)), br_recv.at[k])
+        dst = piece(k, zl, ma, part(k))
+        send(src, dst, z_send.at[k], zl_recv.at[k], z_peer(1))
+        send(src, dst, z_send.at[k], zr_recv.at[k], z_peer(7))
+
+    def spread(k, shard):
+        src = piece(k, shard, ma, part(k))
+        send(src, src, a_send.at[k], al_recv.at[k], a_peer(1))
+        send(src, src, a_send.at[k], ar_recv.at[k], a_peer(3))
+
+    def stage_1(k):
+        if k + WINDOW < NC:
+            stage_0(k + WINDOW)
+        for recv, relay, shard, which, step in ((zl_recv, zf_recv, down_z, 0, 1), (zr_recv, zg_recv, up_z, 1, 7)):
+            wait(some(k, 1, part(k)), recv.at[k])
+            src = piece(k, shard, ma, part(k, which))
+            send(src, src, z2_send.at[k], relay.at[k], z_peer(step))
+            if CHUNKS[k][3]:
+                spread(k, shard)
+
+    def stage_2(k):
+        wait(some(k, 1, part(k, 0)), zf_recv.at[k])
+        wait(some(k, 1, part(k, 1)), zg_recv.at[k])
+        if CHUNKS[k][3]:
+            spread(k, opposite)
+
+    def stage_3(k):
+        if not CHUNKS[k][3]:
+            return
+        for recv, relay, step, which in ((al_recv, bl_recv, 1, 0), (ar_recv, br_recv, 3, 1)):
+            wait(some(k, 3, part(k)), recv.at[k])
+            for shard in (up_z, opposite, down_z):
+                src = piece(k, shard, lax.rem(ma + 4 - step, 4), part(k, which))
+                send(src, src, b_send.at[k], relay.at[k], a_peer(step))
+
+    def stage_4(k):
+        if CHUNKS[k][3]:
+            wait(some(k, 3, part(k, 0)), bl_recv.at[k])
+            wait(some(k, 3, part(k, 1)), br_recv.at[k])
         send(core_half(k, c), core_half(k, c), c_send.at[k], c_recv.at[k], sibling)
 
-    def stage_d(k):
+    def stage_5(k):
         wait(core_half(k, 0), c_recv.at[k])
 
-    progress = [0]
-
-    def pump(upto):
-        while progress[0] < upto:
-            t = progress[0]
-            if t < NC:
-                stage_a(t)
-            if 0 <= t - 1 < NC:
-                stage_b(t - 1)
-            if 0 <= t - 2 < NC:
-                stage_c(t - 2)
-            progress[0] = t + 1
-
-    def ready(k):
-        pump(min(k + 4, NC + 2))
-        stage_d(k)
+    for k in range(WINDOW):
+        stage_0(k)
 
     def share_left(which):
         cols = pl.ds(pl.multiple_of(c * T, T), T)
         send(tr.at[which, :, oc], lt.at[which, :, :, cols], x_send.at[which], x_recv.at[which], sibling)
         lt[which, :, :, cols] = tr[which, :, c]
 
-    pump(1)
     share_left(0)
 
     lane = lax.broadcasted_iota(jnp.int32, (1, 128), 1)
@@ -227,68 +286,77 @@
         iv[:, lanes(h * 128)] = inv
         ms[:, lanes(h * 128)] = mixed.astype(BF)
 
-    def pairs(fn, first, last):
-        def two(i, carry):
-            fn(2 * i)
-            fn(2 * i + 1)
-            return carry
-
-        lax.fori_loop(first // 2, last // 2, two, 0)
-
     def weights(k, first, count):
         if CHUNKS[k][0]:
             return Wt[:, :, :, first : first + count].reshape(DT, count)
         return Ws[:, :, :, first : first + count].reshape(DS, count)
 
-    for k in range(7):
-        ready(k)
-        _, first, count = CHUNKS[k]
-        for n in range(first, first + count, 256):
-            at[:, n : n + 256] = mm(nt[...], weights(k, n, 256)).astype(BF)
-    for part in range(3):
-        pairs(teacher_pair, 4 * part, 4 * part + 4)
-        pump(min(progress[0] + 1, NC + 2))
-    for k in range(7, 10):
-        ready(k)
-        _, first, count = CHUNKS[k]
-        for n in range(first, first + count, 256):
-            as_[:, n : n + 256] = mm(ns[...], weights(k, n, 256)).astype(BF)
-    for part in range(2):
-        pairs(student_pair, 4 * part, 4 * part + 4)
-        pump(min(progress[0] + 1, NC + 2))
-    tr[1] = ms[...].astype(F32).T.astype(BF).reshape(8, 2, 64, T)
-    share_left(1)
-
-    ready(10)
-    square = jnp.zeros((T, 1), F32)
-    for n in range(0, DS, 256):
-        res = xs[:, n : n + 256].astype(F32) + mm(ms[...], weights(10, 3072 + n, 256))
-        square += jnp.sum(res * res, axis=-1, keepdims=True)
+    state = {}
+
+    def tiles(k):
+        _, first, count, _ = CHUNKS[k]
+        return range(first, first + count, 256)
+
+    def project_teacher(k, n):
+        at[:, n : n + 256] = mm(nt[...], weights(k, n, 256)).astype(BF)
+
+    def project_student(k, n):
+        as_[:, n : n + 256] = mm(ns[...], weights(k, n, 256)).astype(BF)
+
+    def share_mixed():
+        tr[1] = ms[...].astype(F32).T.astype(BF).reshape(8, 2, 64, T)
+        share_left(1)
+
+    def result(k, n):
+        n = n - 3 * DS
+        res = xs[:, n : n + 256].astype(F32) + mm(ms[...], weights(k, 3 * DS + n, 256))
+        square = jnp.sum(res * res, axis=-1, keepdims=True)
         rs[:, n : n + 256] = res
-    scale = lax.rsqrt(square / DS + EPS) * DS**-0.5
-    for n in range(0, DS, 256):
-        unit = rs[:, n : n + 256] * scale
-        rs[:, n : n + 256] = unit
-        high = unit.astype(BF)
-        uh_ref[:, n : n + 256] = high
-        ul_ref[:, n : n + 256] = (unit - high.astype(F32)).astype(BF)
-    cross = mm(uh_ref[...], ul_ref[...], 1, 1)
-    gs[...] = mm(uh_ref[...], uh_ref[...], 1, 1) + (cross + cross.T)
-
-    square = jnp.zeros((T, 1), F32)
-    for k in (11, 12, 13):
-        ready(k)
-        _, first, count = CHUNKS[k]
-        for n in range(first, first + count, 256):
-            cols = slice(n - 4608, n - 4608 + 256)
-            feats = (xt[:, cols].astype(F32) + mm(mt[...], weights(k, n, 256))).astype(BF)
-            wide = feats.astype(F32)
-            square += jnp.sum(wide * wide, axis=-1, keepdims=True)
-            term = mm(feats, feats, 1, 1)
-            if n == 4608:
-                gt[...] = term
-            else:
-                gt[...] += term
+        state["result"] = square if n == 0 else state["result"] + square
+
+    def student_unit():
+        state["scale"] = lax.rsqrt(state["result"] / DS + EPS) * DS**-0.5
+        for n in range(0, DS, 256):
+            unit = rs[:, n : n + 256] * state["scale"]
+            rs[:, n : n + 256] = unit
+            high = unit.astype(BF)
+            uh_ref[:, n : n + 256] = high
+            ul_ref[:, n : n + 256] = (unit - high.astype(F32)).astype(BF)
+
+    def student_cross():
+        cross = mm(uh_ref[...], ul_ref[...], 1, 1)
+        gs[...] = cross + cross.T
+
+    def student_gram():
+        gs[...] += mm(uh_ref[...], uh_ref[...], 1, 1)
+
+    def features(k, n):
+        cols = slice(n - 4608, n - 4608 + 256)
+        feats = (xt[:, cols].astype(F32) + mm(mt[...], weights(k, n, 256))).astype(BF)
+        wide = feats.astype(F32)
+        square = jnp.sum(wide * wide, axis=-1, keepdims=True)
+        term = mm(feats, feats, 1, 1)
+        gt[...] = term if n == 4608 else gt[...] + term
+        state["square"] = square if n == 4608 else state["square"] + square
+
+    bind = functools.partial
+    tasks = (
+        [(k, 0.1, bind(project_teacher, k, n)) for k in range(7) for n in tiles(k)]
+        + [(None, 0.35, bind(teacher_pair, h)) for h in range(12)]
+        + [(k, 0.15, bind(project_student, k, n)) for k in range(7, 10) for n in tiles(k)]
+        + [(None, 0.4, bind(student_pair, h)) for h in range(8)]
+        + [(None, 0.5, share_mixed)]
+        + [(10, 0.25, bind(result, 10, n)) for n in tiles(10)]
+        + [(None, 0.5, student_unit), (None, 0.4, student_cross), (None, 0.2, student_gram)]
+        + [(k, 0.4, bind(features, k, n)) for k in range(11, NC) for n in tiles(k)]
+    )
+    steps = {1: stage_1, 2: stage_2, 3: stage_3, 4: stage_4, 5: stage_5}
+    for stage, index in plan([task[:2] for task in tasks]):
+        if stage:
+            steps[stage](index)
+        else:
+            tasks[index][2]()
+    scale, square = state["scale"], state["square"]
     row = lax.rsqrt(square / DT + EPS) * DT**-0.5
     along = jnp.broadcast_to(row, (T, 128)).T[0:1, :]
     diff = 8.0 * (gs[...] - gt[...] * row * along)
@@ -439,9 +507,11 @@
     out[...] = acc
 
     for k in range(NC):
-        wait(three(k, whole(k)), zs_send.at[k])
-        wait(six(k, whole(k)), a_send.at[k])
-        wait(six(k, half(k, 0)), b_send.at[k])
+        wait(some(k, 2, part(k)), z_send.at[k])
+        wait(some(k, 1, part(k)), z2_send.at[k])
+        if CHUNKS[k][3]:
+            wait(some(k, 6, part(k)), a_send.at[k])
+            wait(some(k, 6, part(k, 0)), b_send.at[k])
         wait(core_half(k, 0), c_send.at[k])
     wait(lt.at[0, :, :, 0:T], x_send.at[0])
     wait(lt.at[1, :, :, 0:T], x_send.at[1])
@@ -506,7 +576,7 @@
             vmem((8, 64, 256), BF),
             vmem((7, 64, 256), BF),
             dma((5,)),
-            dma((NC,)), dma((NC,)),
+            dma((NC,)), dma((NC,)), dma((NC,)), dma((NC,)), dma((NC,)), dma((NC,)),
             dma((NC,)), dma((NC,)), dma((NC,)),
             dma((NC,)), dma((NC,)), dma((NC,)),
             dma((NC,)), dma((NC,)),

time: 121 us -> 113 us (0.934)
  Pallas kernels: 119 us -> 112 us
    pallas_call x1, Pallas kernels: 119 us -> 112 us  [per_device(): pl.pallas_call(kernel, out_shape=jax.ShapeDtypeStruct((64, 256), F32), in...]
where the time goes in v3:
time: 113 us
  Pallas kernels  112 us (99%)
  local copies, waits for them, and re-layouts  1.47 us (1%)
    pallas_call x1, Pallas kernels, per_device(): pl.pallas_call(kernel, out_shape=jax.ShapeDtypeStruct((64, 256), F32), in...  112 us

profile of v3, /device:TPU:4, one launch (start us, length us, event | category | flops | bytes accessed | tf_op | source)
XLA Modules:
  0.0 113.0 jit_solution(1617451556288560945)
XLA Ops:
  0.0 111.5 %distill.1 = f32[64,256]{1,0:T(8,128)} custom-call(bf16[512,1536]{1,0:T(8,128)(2,1)} %tt.1, bf16[192,4608]{1,0:T(8,128)(2,1)} %tq.1, bf16[192,1536]{1,0:T(8,128)(2,1)} %to.1, bf16[512,1024]{1,0:T(8,128)(2,1)} %st.1, bf16[128,4096]{1,0:T(8,128)(2,1)} %sw.1), custom_call_target="tpu_custom_call" | custom-call | flops 11399999488 | bytes 30000000 | tf_op jit(solution)/shard_map/distill/pallas_call | solution.py:543
  111.5 1.5 %copy.7 = f32[64,256]{1,0:T(8,128)} copy(f32[64,256]{1,0:T(8,128)} %distill.1) | data formatting | bytes 131072

commit v4 on v3

--- a/solution.py
+++ b/solution.py
@@ -200,6 +200,8 @@
         else:
             src = to.at[rows, slice(first - 4608, first - 4608 + count)]
         dst = piece(k, zl, ma, part(k))
+        mine = buffer(k).at[zl, c, :, part(k)]
+        send(mine, mine, c_send.at[k], c_recv.at[k], sibling)
         send(src, dst, z_send.at[k], zl_recv.at[k], z_peer(1))
         send(src, dst, z_send.at[k], zr_recv.at[k], z_peer(7))
 
@@ -237,7 +239,9 @@
         if CHUNKS[k][3]:
             wait(some(k, 3, part(k, 0)), bl_recv.at[k])
             wait(some(k, 3, part(k, 1)), br_recv.at[k])
-        send(core_half(k, c), core_half(k, c), c_send.at[k], c_recv.at[k], sibling)
+        for shard in (down_z, opposite, up_z):
+            src = buffer(k).at[shard, c, :, part(k)]
+            send(src, src, c_send.at[k], c_recv.at[k], sibling)
 
     def stage_5(k):
         wait(core_half(k, 0), c_recv.at[k])
@@ -340,15 +344,19 @@
         state["square"] = square if n == 4608 else state["square"] + square
 
     bind = functools.partial
+
+    def chunks(teacher, first, last):
+        return [k for k in range(NC) if CHUNKS[k][0] == teacher and first <= CHUNKS[k][1] < last]
+
     tasks = (
-        [(k, 0.1, bind(project_teacher, k, n)) for k in range(7) for n in tiles(k)]
+        [(k, 0.1, bind(project_teacher, k, n)) for k in chunks(True, 0, 3 * DT) for n in tiles(k)]
         + [(None, 0.35, bind(teacher_pair, h)) for h in range(12)]
-        + [(k, 0.15, bind(project_student, k, n)) for k in range(7, 10) for n in tiles(k)]
+        + [(k, 0.15, bind(project_student, k, n)) for k in chunks(False, 0, 3 * DS) for n in tiles(k)]
         + [(None, 0.4, bind(student_pair, h)) for h in range(8)]
         + [(None, 0.5, share_mixed)]
-        + [(10, 0.25, bind(result, 10, n)) for n in tiles(10)]
+        + [(k, 0.25, bind(result, k, n)) for k in chunks(False, 3 * DS, 4 * DS) for n in tiles(k)]
         + [(None, 0.5, student_unit), (None, 0.4, student_cross), (None, 0.2, student_gram)]
-        + [(k, 0.4, bind(features, k, n)) for k in range(11, NC) for n in tiles(k)]
+        + [(k, 0.4, bind(features, k, n)) for k in chunks(True, 3 * DT, 4 * DT) for n in tiles(k)]
     )
     steps = {1: stage_1, 2: stage_2, 3: stage_3, 4: stage_4, 5: stage_5}
     for stage, index in plan([task[:2] for task in tasks]):
@@ -363,9 +371,12 @@
 
     eh = diff.astype(BF)
     el = (diff - eh.astype(F32)).astype(BF)
-    du = mm(eh, uh_ref[...]) + mm(jnp.concatenate([eh, el], axis=1), jnp.concatenate([ul_ref[...], uh_ref[...]], axis=0))
-    unit = rs[...]
-    rg[c, :, 3072:4096] = (scale * (du - jnp.sum(du * unit, axis=-1, keepdims=True) * unit)).astype(BF)
+    along_unit = jnp.sum(diff * gs[...], axis=-1, keepdims=True)
+    for n in range(0, DS, 256):
+        cols = slice(n, n + 256)
+        wide = jnp.concatenate([ul_ref[:, cols], uh_ref[:, cols]], axis=0)
+        du = mm(eh, uh_ref[:, cols]) + mm(jnp.concatenate([eh, el], axis=1), wide)
+        rg[c, :, 3072 + n : 3328 + n] = (scale * (du - along_unit * rs[:, cols])).astype(BF)
     own_out = rg.at[c, :, 3072:4096]
     send(own_out, own_out, x_send.at[2], x_recv.at[2], sibling)
 

time: 113 us -> 112 us (level)
  Pallas kernels: 112 us -> 110 us
    pallas_call x1, Pallas kernels: 112 us -> 110 us  [per_device(): pl.pallas_call(kernel, out_shape=jax.ShapeDtypeStruct((64, 256), F32), in...]
where the time goes in v4:
time: 112 us
  Pallas kernels  110 us (98%)
  local copies, waits for them, and re-layouts  1.47 us (1%)
    pallas_call x1, Pallas kernels, per_device(): pl.pallas_call(kernel, out_shape=jax.ShapeDtypeStruct((64, 256), F32), in...  110 us

profile of v4, /device:TPU:4, one launch (start us, length us, event | category | flops | bytes accessed | tf_op | source)
XLA Modules:
  0.0 111.6 jit_solution(14752214436933809813)
XLA Ops:
  0.0 110.1 %distill.1 = f32[64,256]{1,0:T(8,128)} custom-call(bf16[512,1536]{1,0:T(8,128)(2,1)} %tt.1, bf16[192,4608]{1,0:T(8,128)(2,1)} %tq.1, bf16[192,1536]{1,0:T(8,128)(2,1)} %to.1, bf16[512,1024]{1,0:T(8,128)(2,1)} %st.1, bf16[128,4096]{1,0:T(8,128)(2,1)} %sw.1), custom_call_target="tpu_custom_call" | custom-call | flops 11399999488 | bytes 30000000 | tf_op jit(solution)/shard_map/distill/pallas_call | solution.py:554
  110.1 1.5 %copy.7 = f32[64,256]{1,0:T(8,128)} copy(f32[64,256]{1,0:T(8,128)} %distill.1) | data formatting | bytes 131072
